TPU v7x, 32 devices: a whole 2x2x4 slice. The times are simulated.
32 devices in a mesh: clip: 2 (over x), frame: 16 (over z, y, core).
Axes of the slice: x: 2, y: 2, z: 4, core: 2. Of those that a mesh axis runs over, the one named last changes fastest.
Arguments:
- queries: bfloat16 [16384, 2560], P(('clip', 'frame')), parts along dimension 0, may hold values from -12 to 12
- key_rows: bfloat16 [16384, 2560], P(('clip', 'frame')), parts along dimension 0, may hold values from -12 to 12
- values: bfloat16 [16384, 2560], P(('clip', 'frame')), parts along dimension 0, may hold values from -6 to 6
- block_lists: int32 [128, 8], P(('clip', 'frame')), parts along dimension 0, may hold values from -1 to 63, as said below
Outputs:
- attended: bfloat16 [16384, 2560], P(('clip', 'frame')), parts along dimension 0
There are 2 independent parts, one for each index of `clip`. A program takes and returns all parts, laid end to end along the dimension named above; each array names one. Nothing has to cross between parts.
Inputs may be any that keep to these rules, and one draw needn't show every extreme that they name: `block_lists`: each row names distinct blocks in no particular order, -1 marking an empty slot. Row r names every block of its own device j = r // 4 (blocks 4 * j to 4 * j + 3) and otherwise only blocks of devices at most 2 away. Over the 4 rows of one device, the blocks named that lie on any one other device number at most 1.
All inputs are finite; a program needn't handle non-finite values.
Results may differ from a plain program's by a relative error of at most 0.0046.
Values may be sent and summed in bfloat16 or wider, within the bound.
A program may use at most 128 MiB of HBM per device.

v0:
```python
import jax
import jax.numpy as jnp
from jax import lax
from jax.sharding import PartitionSpec as P

HD = 128
REACH = 2


def shifted(block, axis, distance):
    devices = range(lax.axis_size(axis))
    route = [(i - distance, i) for i in devices if i - distance in devices]
    return lax.ppermute(block, axis, route)


def offsets_list():
    result = []
    for distance in range(1, REACH + 1):
        result.append(-distance)
        result.append(distance)
    return result


def local(queries, key_rows, values, block_lists):
    per_device = block_lists.shape[0]
    tok_rows = queries.shape[0]
    row_width = queries.shape[1]
    block_rows = tok_rows // per_device
    device = lax.axis_index("frame")
    devices_total = lax.axis_size("frame")
    local_range = jnp.arange(per_device, dtype=jnp.int32)
    pool_keys = [key_rows]
    pool_values = [values]
    pool_ids = [device * per_device + local_range]
    for offset in offsets_list():
        moved_keys, moved_values = shifted((key_rows, values), "frame", -offset)
        target = device + offset
        inside = (target >= 0) & (target < devices_total)
        pool_keys.append(moved_keys)
        pool_values.append(moved_values)
        pool_ids.append(jnp.where(inside, target * per_device + local_range, -1))
    all_keys = jnp.concatenate(pool_keys, axis=0)
    all_values = jnp.concatenate(pool_values, axis=0)
    all_ids = jnp.concatenate(pool_ids, axis=0)
    pool_blocks = all_ids.shape[0]
    named_mask = (
        jnp.any(block_lists[:, :, None] == all_ids[None, None, :], axis=1) & (all_ids >= 0)[None, :]
    )
    full_mask = jnp.broadcast_to(
        named_mask[:, None, :, None], (per_device, block_rows, pool_blocks, block_rows)
    ).reshape(tok_rows, pool_blocks * block_rows)
    score_scale = HD ** (-0.5)
    head_count = row_width // HD

    def head_step(head_index, output):
        start = head_index * HD
        query_head = lax.dynamic_slice_in_dim(queries, start, HD, 1)
        key_head = lax.dynamic_slice_in_dim(all_keys, start, HD, 1)
        value_head = lax.dynamic_slice_in_dim(all_values, start, HD, 1)
        scores = (
            lax.dot_general(
                query_head, key_head, (((1,), (1,)), ((), ())), preferred_element_type=jnp.float32
            )
            * score_scale
        )
        scores = jnp.where(full_mask, scores, -jnp.inf)
        row_peak = jnp.max(scores, axis=1, keepdims=True)
        weights = jnp.where(full_mask, jnp.exp(scores - row_peak), 0.0)
        row_total = jnp.sum(weights, axis=1, keepdims=True)
        attended = (
            jnp.dot(weights.astype(jnp.bfloat16), value_head, preferred_element_type=jnp.float32)
            / row_total
        )
        return lax.dynamic_update_slice_in_dim(output, attended.astype(jnp.bfloat16), start, 1)

    output = jnp.zeros((tok_rows, row_width), jnp.bfloat16)
    return lax.fori_loop(0, head_count, head_step, output)


def solution(mesh):
    return jax.shard_map(
        local,
        mesh=mesh,
        in_specs=(
            P(("clip", "frame"), None),
            P(("clip", "frame"), None),
            P(("clip", "frame"), None),
            P(("clip", "frame"), None),
        ),
        out_specs=P(("clip", "frame"), None),
        check_vma=False,
    )
```

profile of v0, /device:TPU:11, one launch (start us, length us, event | category | flops | bytes accessed | tf_op | source)
XLA Modules:
  0.0 525.4 jit_solution(15552923086181212458)
XLA Ops:
  0.0 4.0 collective-permute-start
  5.9 3.2 collective-permute-start.2
  9.1 3.0 collective-permute-start.3
  12.1 3.7 collective-permute-start.4
  16.0 3.4 constant_dynamic-update-slice_fusion.4
  21.0 147.5 %collective-permute-done = bf16[512,2560]{1,0:T(8,128)(2,1)} collective-permute-done((bf16[512,2560]{1,0:T(8,128)(2,1)}, bf16[512,2560]{1,0:T(8,128)(2,1)}, u32[]{:S(2)}, u32[]{:S(2)}) %collective-permute-start) | collective-permute-done | bytes 2621472 | tf_op jit(solution)/shard_map/ppermute | solution.py:13
  170.5 4.2 collective-permute-done.1
  176.8 76.0 %collective-permute-done.2 = bf16[512,2560]{1,0:T(8,128)(2,1)} collective-permute-done((bf16[512,2560]{1,0:T(8,128)(2,1)}, bf16[512,2560]{1,0:T(8,128)(2,1)}, u32[]{:S(2)}, u32[]{:S(2)}) %collective-permute-start.2) | collective-permute-done | bytes 2621472 | tf_op jit(solution)/shard_map/ppermute | solution.py:13
  252.8 4.0 collective-permute-start.7
  256.8 3.4 constant_dynamic-update-slice_fusion.3
  260.2 3.5 constant_dynamic-update-slice_fusion.2
  263.7 4.2 constant_dynamic-update-slice_fusion.1
  267.9 3.5 constant_dynamic-update-slice_fusion
  271.3 42.4 %collective-permute-done.4 = bf16[512,2560]{1,0:T(8,128)(2,1)} collective-permute-done((bf16[512,2560]{1,0:T(8,128)(2,1)}, bf16[512,2560]{1,0:T(8,128)(2,1)}, u32[]{:S(2)}, u32[]{:S(2)}) %collective-permute-start.4) | collective-permute-done | bytes 2621472 | tf_op jit(solution)/shard_map/ppermute | solution.py:13
  317.6 24.1 %collective-permute-done.6 = bf16[512,2560]{1,0:T(8,128)(2,1)} collective-permute-done((bf16[512,2560]{1,0:T(8,128)(2,1)S(1)}, bf16[512,2560]{1,0:T(8,128)(2,1)}, u32[]{:S(2)}, u32[]{:S(2)}) %collective-permute-start.6) | collective-permute-done | bytes 2621472 | tf_op jit(solution)/shard_map/ppermute | solution.py:13
  344.0 4.5 copy-done.3
  348.5 175.4 %while.14 = (s32[]{:T(128)}, bf16[512,2560]{1,0:T(8,128)(2,1)S(1)}, bf16[512,2560]{1,0:T(8,128)(2,1)}, bf16[2560,2560]{1,0:T(8,128)(2,1)}, bf16[2560,2560]{1,0:T...) while((s32[]{:T(128)}, bf16[512,2560]{1,0:T(8,128)(2,1)S(1)}, ...), condition=%wide.region_4.5_spmd.clone, body=%wide.region_1.4_spmd.clone.sunk | while | flops 683015168 | bytes 27799780 | solution.py:77
  351.3 2.3 fusion.31
  355.0 2.3 fusion.33
  360.1 2.3 fusion.31
  363.7 2.3 fusion.33
  368.9 2.3 fusion.31
  377.7 2.3 fusion.31
  386.5 2.3 fusion.31
  390.1 2.3 fusion.33
  395.2 2.3 fusion.31
  398.9 2.3 fusion.33
  404.0 2.3 fusion.31
  407.6 2.4 fusion.33
  412.8 2.3 fusion.31
  421.6 2.3 fusion.31
  430.4 2.3 fusion.31
  434.0 2.3 fusion.33
  439.1 2.3 fusion.31
  442.8 2.3 fusion.33
  447.9 2.3 fusion.31
  456.7 2.3 fusion.31
  460.3 2.3 fusion.33
  465.4 2.3 fusion.31
  474.2 2.3 fusion.31
  483.0 2.3 fusion.31
  486.6 2.3 fusion.33
  491.7 2.3 fusion.31
  495.4 2.3 fusion.33
  500.5 2.3 fusion.31
  504.1 2.3 fusion.33
  509.3 2.3 fusion.31
  518.0 2.3 fusion.31
  (118 shorter events, 118.7 us)
Async XLA Ops:
  0.0 19.4 %copy-start = (bf16[512,2560]{1,0:T(8,128)(2,1)S(1)}, bf16[512,2560]{1,0:T(8,128)(2,1)}, u32[]{:S(2)}) copy-start(bf16[512,2560]{1,0:T(8,128)(2,1)} %param.8) | copy-start | bytes 7864324
  0.0 168.5 %collective-permute-start = (bf16[512,2560]{1,0:T(8,128)(2,1)}, bf16[512,2560]{1,0:T(8,128)(2,1)}, u32[]{:S(2)}, u32[]{:S(2)}) collective-permute-start(bf16[512,2560]{1,0:T(8,128)(2,1)} %param.7), channel_id=1, source_target_pairs={{0,1},{1,2},{2,3},{3,4},{4,5},{5,6},{6,7},{7,8},{8,9},{9,10},{10,1... | collective-permute-start | bytes 7864328 | tf_op jit(solution)/shard_map/ppermute | solution.py:13
  4.0 170.8 %collective-permute-start.1 = (bf16[512,2560]{1,0:T(8,128)(2,1)}, bf16[512,2560]{1,0:T(8,128)(2,1)}, u32[]{:S(2)}, u32[]{:S(2)}) collective-permute-start(bf16[512,2560]{1,0:T(8,128)(2,1)} %param.7), channel_id=1, source_target_pairs={{1,0},{2,1},{3,2},{4,3},{5,4},{6,5},{7,6},{8,7},{9,8},{10,9},{11,1... | collective-permute-start | bytes 7864328 | tf_op jit(solution)/shard_map/ppermute | solution.py:13
  5.9 246.9 %collective-permute-start.2 = (bf16[512,2560]{1,0:T(8,128)(2,1)}, bf16[512,2560]{1,0:T(8,128)(2,1)}, u32[]{:S(2)}, u32[]{:S(2)}) collective-permute-start(bf16[512,2560]{1,0:T(8,128)(2,1)} %param.7), channel_id=1, source_target_pairs={{0,2},{1,3},{2,4},{3,5},{4,6},{5,7},{6,8},{7,9},{8,10},{9,11},{10,... | collective-permute-start | bytes 7864328 | tf_op jit(solution)/shard_map/ppermute | solution.py:13
  9.1 258.8 %collective-permute-start.3 = (bf16[512,2560]{1,0:T(8,128)(2,1)}, bf16[512,2560]{1,0:T(8,128)(2,1)}, u32[]{:S(2)}, u32[]{:S(2)}) collective-permute-start(bf16[512,2560]{1,0:T(8,128)(2,1)} %param.7), channel_id=1, source_target_pairs={{2,0},{3,1},{4,2},{5,3},{6,4},{7,5},{8,6},{9,7},{10,8},{11,9},{12,... | collective-permute-start | bytes 7864328 | tf_op jit(solution)/shard_map/ppermute | solution.py:13
  12.1 301.6 %collective-permute-start.4 = (bf16[512,2560]{1,0:T(8,128)(2,1)}, bf16[512,2560]{1,0:T(8,128)(2,1)}, u32[]{:S(2)}, u32[]{:S(2)}) collective-permute-start(bf16[512,2560]{1,0:T(8,128)(2,1)} %param.8), channel_id=1, source_target_pairs={{0,1},{1,2},{2,3},{3,4},{4,5},{5,6},{6,7},{7,8},{8,9},{9,10},{10,1... | collective-permute-start | bytes 7864328 | tf_op jit(solution)/shard_map/ppermute | solution.py:13
  16.0 154.5 %copy-start.4 = (s32[4,8]{1,0:T(4,128)S(1)}, s32[4,8]{1,0:T(4,128)}, u32[]{:S(2)}) copy-start(s32[4,8]{1,0:T(4,128)} %param.9) | copy-start | bytes 388
  168.5 147.2 %collective-permute-start.5 = (bf16[512,2560]{1,0:T(8,128)(2,1)S(1)}, bf16[512,2560]{1,0:T(8,128)(2,1)}, u32[]{:S(2)}, u32[]{:S(2)}) collective-permute-start(bf16[512,2560]{1,0:T(8,128)(2,1)S(1)} %copy-done), channel_id=1, source_target_pairs={{1,0},{2,1},{3,2},{4,3},{5,4},{6,5},{7,6},{8,7},{9,8},{10,9},{11,1... | collective-permute-start | bytes 7864328 | tf_op jit(solution)/shard_map/ppermute | solution.py:13
  174.8 167.0 %collective-permute-start.6 = (bf16[512,2560]{1,0:T(8,128)(2,1)S(1)}, bf16[512,2560]{1,0:T(8,128)(2,1)}, u32[]{:S(2)}, u32[]{:S(2)}) collective-permute-start(bf16[512,2560]{1,0:T(8,128)(2,1)S(1)} %copy-done), channel_id=1, source_target_pairs={{0,2},{1,3},{2,4},{3,5},{4,6},{5,7},{6,8},{7,9},{8,10},{9,11},{10,... | collective-permute-start | bytes 7864328 | tf_op jit(solution)/shard_map/ppermute | solution.py:13
  252.8 90.9 %collective-permute-start.7 = (bf16[512,2560]{1,0:T(8,128)(2,1)S(1)}, bf16[512,2560]{1,0:T(8,128)(2,1)S(1)}, u32[]{:S(2)}, u32[]{:S(2)}) collective-permute-start(bf16[512,2560]{1,0:T(8,128)(2,1)S(1)} %copy-done), channel_id=1, source_target_pairs={{2,0},{3,1},{4,2},{5,3},{6,4},{7,5},{8,6},{9,7},{10,8},{11,9},{12,... | collective-permute-start | bytes 7864328 | tf_op jit(solution)/shard_map/ppermute | solution.py:13
  260.2 53.6 %copy-start.2 = (bf16[2560,2560]{1,0:T(8,128)(2,1)S(1)}, bf16[2560,2560]{1,0:T(8,128)(2,1)}, u32[]{:S(2)}) copy-start(bf16[2560,2560]{1,0:T(8,128)(2,1)} %constant_dynamic-update-slice_fusion.9) | copy-start | bytes 39321604
  343.8 4.7 copy-start.3
  523.9 1.5 copy-start.1
where the time goes:
time: 528 us; the launch traced here: 525 us
  waiting for transfers between devices  294 us (56%)
  matrix products  91.8 us (17%)
  local copies, waits for them, and re-layouts  88 us (17%)
  other arithmetic  26.8 us (5%)
  starting transfers between devices  23.6 us (4%)
    ppermute x8, waiting for transfers between devices, shifted(): return lax.ppermute(block, axis, route)  294 us
    dot_general x20, matrix products, head_step(): lax.dot_general(query_head, key_head, (((1,), (1,)), ((), ())), preferred...  45.9 us
    dot_general x20, matrix products, head_step(): jnp.dot(weights.astype(jnp.bfloat16), value_head, preferred_element_type=...  45.8 us
    reshape x20, local copies, waits for them, and re-layouts, local(): full_mask = jnp.broadcast_to(named_mask[:, None, :, None], (per_device, b...  28.5 us
    unnamed x19, local copies, waits for them, and re-layouts  28 us
    reduce_sum x20, other arithmetic, head_step(): row_total = jnp.sum(weights, axis=1, keepdims=True)  26.7 us
    ppermute x8, starting transfers between devices, shifted(): return lax.ppermute(block, axis, route)  23.6 us
    broadcast_in_dim x20, local copies, waits for them, and re-layouts, local(): jnp.broadcast_to(named_mask[:, None, :, None], (per_device, block_rows, p...  14.8 us
  transfers between devices with their start and end apart: 8, of which 5 were waited for; matrix products, arithmetic and copies ran while one was open for 5% of the time, Pallas kernels for 0%

commit v1 on v0

v1 whole, which is shorter than its diff:
```python
import functools
import math

import jax
import jax.numpy as jnp
from jax import lax
from jax.experimental import pallas as pl
from jax.experimental.pallas import tpu as pltpu
from jax.sharding import PartitionSpec as P

HD = 128
REACH = 2
GROUP_HEADS = 2
OFFSETS = (-1, 1, -2, 2)
SLOTS = len(OFFSETS)


def kernel(
    size,
    q_hbm,
    k_hbm,
    v_hbm,
    lists_smem,
    lists_vmem,
    out_hbm,
    q_ref,
    k_ref,
    v_ref,
    out_ref,
    named_vmem,
    named_smem,
    send_ref,
    recv_ref,
    acc_ref,
    peak_ref,
    total_ref,
    bias_ref,
    pick_ref,
    load_sem,
    list_send_sem,
    list_recv_sem,
    smem_sem,
    send_sem,
    recv_sem,
    out_sem,
):
    me = lax.axis_index("frame")
    per_device, slots_row = lists_smem.shape
    tokens = q_ref.shape[0]
    block = tokens // per_device
    groups = recv_ref.shape[0]
    group_width = recv_ref.shape[3]
    scale = HD ** (-0.5) * math.log2(math.e)

    def inside(slot):
        other = me + OFFSETS[slot]
        return (other >= 0) & (other < size)

    loads = [
        pltpu.make_async_copy(k_hbm, k_ref, load_sem.at[0]),
        pltpu.make_async_copy(v_hbm, v_ref, load_sem.at[1]),
        pltpu.make_async_copy(q_hbm, q_ref, load_sem.at[2]),
    ]
    for load in loads:
        load.start()

    barrier = pltpu.get_barrier_semaphore()
    count = jnp.int32(0)
    for slot in range(SLOTS):
        present = inside(slot)
        count = count + present.astype(jnp.int32)

        @pl.when(present)
        def _():
            pl.semaphore_signal(
                barrier,
                inc=1,
                device_id={"frame": me + OFFSETS[slot]},
                device_id_type=pl.DeviceIdType.MESH,
            )

    pl.semaphore_wait(barrier, count)

    def list_copy(slot):
        return pltpu.make_async_remote_copy(
            src_ref=lists_vmem,
            dst_ref=named_vmem.at[slot ^ 1],
            send_sem=list_send_sem.at[slot],
            recv_sem=list_recv_sem.at[slot ^ 1],
            device_id={"frame": me + OFFSETS[slot]},
            device_id_type=pl.DeviceIdType.MESH,
        )

    def list_arrival(slot):
        return pltpu.make_async_remote_copy(
            src_ref=lists_vmem,
            dst_ref=named_vmem.at[slot],
            send_sem=list_send_sem.at[slot],
            recv_sem=list_recv_sem.at[slot],
            device_id={"frame": me + OFFSETS[slot]},
            device_id_type=pl.DeviceIdType.MESH,
        )

    for slot in range(SLOTS):

        @pl.when(inside(slot))
        def _():
            list_copy(slot).start()

        @pl.when(jnp.logical_not(inside(slot)))
        def _():
            named_vmem[slot] = jnp.full((per_device, slots_row), -1, jnp.int32)
            for part in range(2):
                recv_ref[:, part, slot * block : (slot + 1) * block, :] = jnp.zeros(
                    (groups, block, group_width), jnp.bfloat16
                )

    for row in range(per_device):
        entries = [lists_smem[row, column] for column in range(slots_row)]
        for slot in range(SLOTS):
            first = (me + OFFSETS[slot]) * per_device
            named = jnp.bool_(False)
            for entry in entries:
                named = named | ((entry >= 0) & (entry >= first) & (entry < first + per_device))
            bias_ref[row * block : (row + 1) * block, slot * block : (slot + 1) * block] = jnp.full(
                (block, block), jnp.where(named, 0.0, -jnp.inf), jnp.float32
            )

    for slot in range(SLOTS):

        @pl.when(inside(slot))
        def _():
            list_arrival(slot).wait_recv()

    to_smem = pltpu.make_async_copy(named_vmem, named_smem, smem_sem)
    to_smem.start()
    to_smem.wait()

    for slot in range(SLOTS):
        chosen = jnp.int32(0)
        for row in range(per_device):
            for column in range(slots_row):
                local_id = named_smem[slot, row, column] - me * per_device
                chosen = jnp.where((local_id >= 0) & (local_id < per_device), local_id, chosen)
        for place in range(per_device):
            pick_ref[slot, place] = jnp.full(
                (block, group_width), jnp.where(chosen == place, 1.0, 0.0), jnp.float32
            ).astype(jnp.bfloat16)

    loads[0].wait()
    loads[1].wait()

    def block_copy(group, slot):
        return pltpu.make_async_remote_copy(
            src_ref=send_ref.at[slot, group],
            dst_ref=recv_ref.at[group, :, pl.ds((slot ^ 1) * block, block), :],
            send_sem=send_sem.at[slot, group],
            recv_sem=recv_sem.at[slot ^ 1, group],
            device_id={"frame": me + OFFSETS[slot]},
            device_id_type=pl.DeviceIdType.MESH,
        )

    def block_arrival(group, slot):
        return pltpu.make_async_remote_copy(
            src_ref=send_ref.at[slot, group],
            dst_ref=recv_ref.at[group, :, pl.ds(slot * block, block), :],
            send_sem=send_sem.at[slot, group],
            recv_sem=recv_sem.at[slot, group],
            device_id={"frame": me + OFFSETS[slot]},
            device_id_type=pl.DeviceIdType.MESH,
        )

    def send_group(group, carry):
        columns = pl.ds(pl.multiple_of(group * group_width, group_width), group_width)
        for slot in (2, 3, 0, 1):

            @pl.when(inside(slot))
            def _():
                for part, source in enumerate((k_ref, v_ref)):
                    picked = source[0:block, columns] * pick_ref[slot, 0]
                    for place in range(1, per_device):
                        rows = slice(place * block, (place + 1) * block)
                        picked = picked + source[rows, columns] * pick_ref[slot, place]
                    send_ref[slot, group, part] = picked
                block_copy(group, slot).start()

        return carry

    lax.fori_loop(0, groups, send_group, 0)

    loads[2].wait()

    def own_head(head, carry):
        columns = pl.ds(pl.multiple_of(head * HD, HD), HD)
        scores = lax.dot_general(
            q_ref[:, columns],
            k_ref[:, columns],
            (((1,), (1,)), ((), ())),
            preferred_element_type=jnp.float32,
        )
        peak = jnp.max(scores, axis=1, keepdims=True)
        weights = jnp.exp2((scores - peak) * scale)
        peak_ref[head] = peak
        total_ref[head] = jnp.sum(weights, axis=1, keepdims=True)
        acc_ref[:, columns] = jnp.dot(
            weights.astype(jnp.bfloat16), v_ref[:, columns], preferred_element_type=jnp.float32
        )
        return carry

    lax.fori_loop(0, groups * GROUP_HEADS, own_head, 0)

    def out_copy(group):
        columns = pl.ds(pl.multiple_of(group * group_width, group_width), group_width)
        return pltpu.make_async_copy(
            out_ref.at[:, columns], out_hbm.at[:, columns], out_sem.at[group]
        )

    def far_group(group, carry):
        for slot in range(SLOTS):

            @pl.when(inside(slot))
            def _():
                block_arrival(group, slot).wait_recv()

        for step in range(GROUP_HEADS):
            head = group * GROUP_HEADS + step
            columns = pl.ds(pl.multiple_of(head * HD, HD), HD)
            far_columns = slice(step * HD, (step + 1) * HD)
            scores = lax.dot_general(
                q_ref[:, columns],
                recv_ref[group, 0, :, far_columns],
                (((1,), (1,)), ((), ())),
                preferred_element_type=jnp.float32,
            )
            scores = scores + bias_ref[...]
            own_peak = peak_ref[head]
            peak = jnp.maximum(jnp.max(scores, axis=1, keepdims=True), own_peak)
            weights = jnp.exp2((scores - peak) * scale)
            shrink = jnp.exp2((own_peak - peak) * scale)
            total = total_ref[head] * shrink + jnp.sum(weights, axis=1, keepdims=True)
            far = jnp.dot(
                weights.astype(jnp.bfloat16),
                recv_ref[group, 1, :, far_columns],
                preferred_element_type=jnp.float32,
            )
            attended = (acc_ref[:, columns] * shrink + far) / total
            out_ref[:, columns] = attended.astype(jnp.bfloat16)
        out_copy(group).start()
        return carry

    lax.fori_loop(0, groups, far_group, 0)

    def finish(group, carry):
        for slot in range(SLOTS):

            @pl.when(inside(slot))
            def _():
                block_copy(group, slot).wait_send()

        out_copy(group).wait()
        return carry

    lax.fori_loop(0, groups, finish, 0)
    for slot in range(SLOTS):

        @pl.when(inside(slot))
        def _():
            list_copy(slot).wait_send()


def local(size, queries, key_rows, values, block_lists):
    tokens, width = queries.shape
    per_device, slots_row = block_lists.shape
    block = tokens // per_device
    heads = width // HD
    groups = heads // GROUP_HEADS
    group_width = GROUP_HEADS * HD
    far = SLOTS * block
    hbm = pl.BlockSpec(memory_space=pl.ANY)
    return pl.pallas_call(
        functools.partial(kernel, size),
        out_shape=jax.ShapeDtypeStruct((tokens, width), jnp.bfloat16),
        in_specs=[
            hbm,
            hbm,
            hbm,
            pl.BlockSpec(memory_space=pltpu.SMEM),
            pl.BlockSpec(memory_space=pltpu.VMEM),
        ],
        out_specs=hbm,
        scratch_shapes=[
            pltpu.VMEM((tokens, width), jnp.bfloat16),
            pltpu.VMEM((tokens, width), jnp.bfloat16),
            pltpu.VMEM((tokens, width), jnp.bfloat16),
            pltpu.VMEM((tokens, width), jnp.bfloat16),
            pltpu.VMEM((SLOTS, per_device, slots_row), jnp.int32),
            pltpu.SMEM((SLOTS, per_device, slots_row), jnp.int32),
            pltpu.VMEM((SLOTS, groups, 2, block, group_width), jnp.bfloat16),
            pltpu.VMEM((groups, 2, far, group_width), jnp.bfloat16),
            pltpu.VMEM((tokens, width), jnp.float32),
            pltpu.VMEM((heads, tokens, 1), jnp.float32),
            pltpu.VMEM((heads, tokens, 1), jnp.float32),
            pltpu.VMEM((tokens, far), jnp.float32),
            pltpu.VMEM((SLOTS, per_device, block, group_width), jnp.bfloat16),
            pltpu.SemaphoreType.DMA((3,)),
            pltpu.SemaphoreType.DMA((SLOTS,)),
            pltpu.SemaphoreType.DMA((SLOTS,)),
            pltpu.SemaphoreType.DMA,
            pltpu.SemaphoreType.DMA((SLOTS, groups)),
            pltpu.SemaphoreType.DMA((SLOTS, groups)),
            pltpu.SemaphoreType.DMA((groups,)),
        ],
        compiler_params=pltpu.CompilerParams(
            collective_id=0, has_side_effects=True, vmem_limit_bytes=56 * 1024 * 1024
        ),
        cost_estimate=pl.CostEstimate(
            flops=4 * tokens * (tokens + far) * width,
            bytes_accessed=4 * tokens * width * 2,
            transcendentals=heads * tokens * (tokens + far),
        ),
    )(queries, key_rows, values, block_lists, block_lists)


def solution(mesh):
    rows = P(("clip", "frame"), None)
    return jax.shard_map(
        functools.partial(local, mesh.shape["frame"]),
        mesh=mesh,
        in_specs=(rows, rows, rows, rows),
        out_specs=rows,
        check_vma=False,
    )
```

time: 528 us -> 104 us (0.20)
  waiting for transfers between devices: 294 us -> 0 us
  Pallas kernels: 0 us -> 100 us
  matrix products: 91.8 us -> 0 us
  local copies, waits for them, and re-layouts: 88 us -> 3.4 us
  other arithmetic: 26.8 us -> 0 us
  starting transfers between devices: 23.6 us -> 0 us
    ppermute x8 -> x0, waiting for transfers between devices: 294 us -> none  [shifted(): return lax.ppermute(block, axis, route)]
    pallas_call x0 -> x1, Pallas kernels: none -> 100 us  [local(): pl.pallas_call(functools.partial(kernel, size), out_shape=jax.ShapeDtypeS...]
    dot_general x40 -> x0, matrix products: 91.8 us -> none  [the longest x20 45.9 us: head_step(): lax.dot_general(query_head, key_head, (((1,), (1,)), ((), ())), preferred...]
    reshape x20 -> x0, local copies, waits for them, and re-layouts: 28.5 us -> none  [local(): full_mask = jnp.broadcast_to(named_mask[:, None, :, None], (per_device, b...]
    reduce_sum x20 -> x0, other arithmetic: 26.7 us -> none  [head_step(): row_total = jnp.sum(weights, axis=1, keepdims=True)]
    unnamed x19 -> x1, local copies, waits for them, and re-layouts: 28 us -> 3.4 us
    ppermute x8 -> x0, starting transfers between devices: 23.6 us -> none  [shifted(): return lax.ppermute(block, axis, route)]
    broadcast_in_dim x21 -> x0, local copies, waits for them, and re-layouts: 15 us -> none  [the longest x20 14.8 us: local(): jnp.broadcast_to(named_mask[:, None, :, None], (per_device, block_rows, p...]
  transfers between devices with their start and end apart: 8 -> 0, of which waited for: 5 -> 0; matrix products, arithmetic and copies ran while one was open for 5% -> 0% of each run, Pallas kernels for 0% -> 0%
where the time goes in v1:
time: 104 us; the launch traced here: 103 us
  Pallas kernels  100 us (96%)
  local copies, waits for them, and re-layouts  3.4 us (3%)
    pallas_call x1, Pallas kernels, local(): pl.pallas_call(functools.partial(kernel, size), out_shape=jax.ShapeDtypeS...  100 us
    unnamed x1, local copies, waits for them, and re-layouts  3.4 us

profile of v1, /device:TPU:11, one launch (start us, length us, event | category | flops | bytes accessed | tf_op | source)
XLA Modules:
  0.0 103.4 jit_solution(8481499305591906446)
XLA Ops:
  0.0 100.0 %shard_map.46 = bf16[512,2560]{1,0:T(8,128)(2,1)} custom-call(bf16[512,2560]{1,0:T(8,128)(2,1)} %q_hbm.1, bf16[512,2560]{1,0:T(8,128)(2,1)} %k_hbm.1, bf16[512,2560]{1,0:T(8,128)(2,1)} %v_hbm.1, s32[4,8]{1,0:T(4,128)} %lists_vmem.1, s32[4,8]{1,0:T(4,128)} %lists_vmem.1), custom_call_target="tpu_custom_call" | custom-call | flops 5368709120 | bytes 10485760 | tf_op jit(solution)/shard_map/pallas_call | solution.py:280
  100.0 3.4 %copy.6 = bf16[512,2560]{1,0:T(8,128)(2,1)} copy(bf16[512,2560]{1,0:T(8,128)(2,1)} %shard_map.46) | data formatting | bytes 5242880

commit v2 on v1

--- a/solution.py
+++ b/solution.py
@@ -10,7 +10,9 @@
 
 HD = 128
 REACH = 2
-GROUP_HEADS = 2
+QUAD = 4
+MOST_QUADS = 4
+GROUP_HEADS = 1
 OFFSETS = (-1, 1, -2, 2)
 SLOTS = len(OFFSETS)
 
@@ -36,12 +38,15 @@
     total_ref,
     bias_ref,
     pick_ref,
+    relay_ref,
     load_sem,
     list_send_sem,
     list_recv_sem,
     smem_sem,
     send_sem,
     recv_sem,
+    relay_recv_sem,
+    forward_sem,
     out_sem,
 ):
     me = lax.axis_index("frame")
@@ -64,10 +69,39 @@
     for load in loads:
         load.start()
 
+    quads = size // QUAD
+    quad = me // QUAD
+    relays = size % QUAD == 0 and quads <= MOST_QUADS
+
+    def by_relay(group, upward):
+        share = jnp.where(upward, quads - 1 - quad, quad)
+        back = groups - 1 - group
+        return (back + 1) * share // quads > back * share // quads
+
+    def relayed(group, slot):
+        other = me + OFFSETS[slot]
+        return (other // QUAD != quad) & by_relay(group, OFFSETS[slot] > 0)
+
+    lower = me % QUAD < QUAD // 2
+    sign = jnp.where(lower, 1, -1)
+
+    def forward_target(flow):
+        return me + sign * (QUAD // 2 + 1 + flow)
+
+    def forwards(group, flow):
+        target = forward_target(flow)
+        return (
+            (target >= 0)
+            & (target < size)
+            & (target // QUAD == quad + sign)
+            & by_relay(group, lower)
+        )
+
     barrier = pltpu.get_barrier_semaphore()
     count = jnp.int32(0)
-    for slot in range(SLOTS):
-        present = inside(slot)
+    span = REACH + QUAD // 2 if relays else REACH
+    for offset in [o for o in range(-span, span + 1) if o]:
+        present = (me + offset >= 0) & (me + offset < size)
         count = count + present.astype(jnp.int32)
 
         @pl.when(present)
@@ -75,7 +109,7 @@
             pl.semaphore_signal(
                 barrier,
                 inc=1,
-                device_id={"frame": me + OFFSETS[slot]},
+                device_id={"frame": me + offset},
                 device_id_type=pl.DeviceIdType.MESH,
             )
 
@@ -170,6 +204,47 @@
             device_id_type=pl.DeviceIdType.MESH,
         )
 
+    def relay_copy(group, slot):
+        step = QUAD // 2 if OFFSETS[slot] < 0 else -(QUAD // 2)
+        flow = abs(OFFSETS[slot]) - 1
+        return pltpu.make_async_remote_copy(
+            src_ref=send_ref.at[slot, group],
+            dst_ref=relay_ref.at[flow, group],
+            send_sem=send_sem.at[slot, group],
+            recv_sem=relay_recv_sem.at[flow, group],
+            device_id={"frame": me + step},
+            device_id_type=pl.DeviceIdType.MESH,
+        )
+
+    def relay_arrival(group, flow):
+        return pltpu.make_async_remote_copy(
+            src_ref=relay_ref.at[flow, group],
+            dst_ref=relay_ref.at[flow, group],
+            send_sem=forward_sem.at[flow, group],
+            recv_sem=relay_recv_sem.at[flow, group],
+            device_id={"frame": forward_target(flow)},
+            device_id_type=pl.DeviceIdType.MESH,
+        )
+
+    def forward_copy(group, flow):
+        slot = 2 * flow + jnp.where(lower, 0, 1)
+        return pltpu.make_async_remote_copy(
+            src_ref=relay_ref.at[flow, group],
+            dst_ref=recv_ref.at[group, :, pl.ds(pl.multiple_of(slot * block, block), block), :],
+            send_sem=forward_sem.at[flow, group],
+            recv_sem=recv_sem.at[slot, group],
+            device_id={"frame": forward_target(flow)},
+            device_id_type=pl.DeviceIdType.MESH,
+        )
+
+    def forward_group(group):
+        for flow in range(REACH):
+
+            @pl.when(forwards(group, flow))
+            def _():
+                relay_arrival(group, flow).wait_recv()
+                forward_copy(group, flow).start()
+
     def send_group(group, carry):
         columns = pl.ds(pl.multiple_of(group * group_width, group_width), group_width)
         for slot in (2, 3, 0, 1):
@@ -182,7 +257,19 @@
                         rows = slice(place * block, (place + 1) * block)
                         picked = picked + source[rows, columns] * pick_ref[slot, place]
                     send_ref[slot, group, part] = picked
-                block_copy(group, slot).start()
+                if relays:
+                    far_way = relayed(group, slot)
+
+                    @pl.when(far_way)
+                    def _():
+                        relay_copy(group, slot).start()
+
+                    @pl.when(jnp.logical_not(far_way))
+                    def _():
+                        block_copy(group, slot).start()
+
+                else:
+                    block_copy(group, slot).start()
 
         return carry
 
@@ -216,6 +303,8 @@
         )
 
     def far_group(group, carry):
+        if relays:
+            forward_group(group)
         for slot in range(SLOTS):
 
             @pl.when(inside(slot))
@@ -256,6 +345,13 @@
             @pl.when(inside(slot))
             def _():
                 block_copy(group, slot).wait_send()
+
+        if relays:
+            for flow in range(REACH):
+
+                @pl.when(forwards(group, flow))
+                def _():
+                    forward_copy(group, flow).wait_send()
 
         out_copy(group).wait()
         return carry
@@ -302,12 +398,15 @@
             pltpu.VMEM((heads, tokens, 1), jnp.float32),
             pltpu.VMEM((tokens, far), jnp.float32),
             pltpu.VMEM((SLOTS, per_device, block, group_width), jnp.bfloat16),
+            pltpu.VMEM((REACH, groups, 2, block, group_width), jnp.bfloat16),
             pltpu.SemaphoreType.DMA((3,)),
             pltpu.SemaphoreType.DMA((SLOTS,)),
             pltpu.SemaphoreType.DMA((SLOTS,)),
             pltpu.SemaphoreType.DMA,
             pltpu.SemaphoreType.DMA((SLOTS, groups)),
             pltpu.SemaphoreType.DMA((SLOTS, groups)),
+            pltpu.SemaphoreType.DMA((REACH, groups)),
+            pltpu.SemaphoreType.DMA((REACH, groups)),
             pltpu.SemaphoreType.DMA((groups,)),
         ],
         compiler_params=pltpu.CompilerParams(

time: 104 us -> 96.2 us (0.925)
  the two profiles are of different devices: /device:TPU:11 before, /device:TPU:4 now
where the time goes in v2:
time: 96.2 us; the launch traced here: 96 us
  Pallas kernels  92.6 us (96%)
  local copies, waits for them, and re-layouts  3.4 us (4%)
    pallas_call x1, Pallas kernels, local(): pl.pallas_call(functools.partial(kernel, size), out_shape=jax.ShapeDtypeS...  92.6 us
    unnamed x1, local copies, waits for them, and re-layouts  3.4 us

profile of v2, /device:TPU:4, one launch (start us, length us, event | category | flops | bytes accessed | tf_op | source)
XLA Modules:
  0.0 96.0 jit_solution(500203751837747996)
XLA Ops:
  0.0 92.6 %shard_map.46 = bf16[512,2560]{1,0:T(8,128)(2,1)} custom-call(bf16[512,2560]{1,0:T(8,128)(2,1)} %q_hbm.1, bf16[512,2560]{1,0:T(8,128)(2,1)} %k_hbm.1, bf16[512,2560]{1,0:T(8,128)(2,1)} %v_hbm.1, s32[4,8]{1,0:T(4,128)} %lists_vmem.1, s32[4,8]{1,0:T(4,128)} %lists_vmem.1), custom_call_target="tpu_custom_call" | custom-call | flops 5368709120 | bytes 10485760 | tf_op jit(solution)/shard_map/pallas_call | solution.py:376
  92.6 3.4 %copy.6 = bf16[512,2560]{1,0:T(8,128)(2,1)} copy(bf16[512,2560]{1,0:T(8,128)(2,1)} %shard_map.46) | data formatting | bytes 5242880

commit v3 on v2

--- a/solution.py
+++ b/solution.py
@@ -12,7 +12,9 @@
 REACH = 2
 QUAD = 4
 MOST_QUADS = 4
-GROUP_HEADS = 1
+FIRST_GROUPS = 2
+OWN_ROWS = 256
+FAR_ROWS = 256
 OFFSETS = (-1, 1, -2, 2)
 SLOTS = len(OFFSETS)
 
@@ -61,6 +63,19 @@
         other = me + OFFSETS[slot]
         return (other >= 0) & (other < size)
 
+    parity = me % 2
+
+    def near(slot):
+        return parity == (1 if OFFSETS[slot] < 0 else 0)
+
+    def place_of(slot):
+        if slot >= 2:
+            return slot * block
+        return pl.multiple_of((1 - parity if slot == 0 else parity) * block, block)
+
+    def place_there(slot):
+        return place_of(slot) if slot < 2 else (slot ^ 1) * block
+
     loads = [
         pltpu.make_async_copy(k_hbm, k_ref, load_sem.at[0]),
         pltpu.make_async_copy(v_hbm, v_ref, load_sem.at[1]),
@@ -75,8 +90,7 @@
 
     def by_relay(group, upward):
         share = jnp.where(upward, quads - 1 - quad, quad)
-        back = groups - 1 - group
-        return (back + 1) * share // quads > back * share // quads
+        return group * quads < groups * share
 
     def relayed(group, slot):
         other = me + OFFSETS[slot]
@@ -145,7 +159,7 @@
         def _():
             named_vmem[slot] = jnp.full((per_device, slots_row), -1, jnp.int32)
             for part in range(2):
-                recv_ref[:, part, slot * block : (slot + 1) * block, :] = jnp.zeros(
+                recv_ref[:, part, pl.ds(place_of(slot), block), :] = jnp.zeros(
                     (groups, block, group_width), jnp.bfloat16
                 )
 
@@ -156,7 +170,7 @@
             named = jnp.bool_(False)
             for entry in entries:
                 named = named | ((entry >= 0) & (entry >= first) & (entry < first + per_device))
-            bias_ref[row * block : (row + 1) * block, slot * block : (slot + 1) * block] = jnp.full(
+            bias_ref[row * block : (row + 1) * block, pl.ds(place_of(slot), block)] = jnp.full(
                 (block, block), jnp.where(named, 0.0, -jnp.inf), jnp.float32
             )
 
@@ -187,7 +201,7 @@
     def block_copy(group, slot):
         return pltpu.make_async_remote_copy(
             src_ref=send_ref.at[slot, group],
-            dst_ref=recv_ref.at[group, :, pl.ds((slot ^ 1) * block, block), :],
+            dst_ref=recv_ref.at[group, :, pl.ds(place_there(slot), block), :],
             send_sem=send_sem.at[slot, group],
             recv_sem=recv_sem.at[slot ^ 1, group],
             device_id={"frame": me + OFFSETS[slot]},
@@ -197,7 +211,7 @@
     def block_arrival(group, slot):
         return pltpu.make_async_remote_copy(
             src_ref=send_ref.at[slot, group],
-            dst_ref=recv_ref.at[group, :, pl.ds(slot * block, block), :],
+            dst_ref=recv_ref.at[group, :, pl.ds(place_of(slot), block), :],
             send_sem=send_sem.at[slot, group],
             recv_sem=recv_sem.at[slot, group],
             device_id={"frame": me + OFFSETS[slot]},
@@ -228,9 +242,10 @@
 
     def forward_copy(group, flow):
         slot = 2 * flow + jnp.where(lower, 0, 1)
+        place = slot * block if flow else block
         return pltpu.make_async_remote_copy(
             src_ref=relay_ref.at[flow, group],
-            dst_ref=recv_ref.at[group, :, pl.ds(pl.multiple_of(slot * block, block), block), :],
+            dst_ref=recv_ref.at[group, :, pl.ds(pl.multiple_of(place, block), block), :],
             send_sem=forward_sem.at[flow, group],
             recv_sem=recv_sem.at[slot, group],
             device_id={"frame": forward_target(flow)},
@@ -245,18 +260,34 @@
                 relay_arrival(group, flow).wait_recv()
                 forward_copy(group, flow).start()
 
-    def send_group(group, carry):
+    def pick(group, slot):
         columns = pl.ds(pl.multiple_of(group * group_width, group_width), group_width)
+        for part, source in enumerate((k_ref, v_ref)):
+            picked = source[0:block, columns] * pick_ref[slot, 0]
+            for choice in range(1, per_device):
+                rows = slice(choice * block, (choice + 1) * block)
+                picked = picked + source[rows, columns] * pick_ref[slot, choice]
+            send_ref[slot, group, part] = picked
+
+    def send_near(group, carry):
+        for slot in (0, 1):
+
+            @pl.when(near(slot) & inside(slot))
+            def _():
+                pick(group, slot)
+                block_copy(group, slot).start()
+
+        return carry
+
+    def send_far(group, carry):
         for slot in (2, 3, 0, 1):
-
-            @pl.when(inside(slot))
-            def _():
-                for part, source in enumerate((k_ref, v_ref)):
-                    picked = source[0:block, columns] * pick_ref[slot, 0]
-                    for place in range(1, per_device):
-                        rows = slice(place * block, (place + 1) * block)
-                        picked = picked + source[rows, columns] * pick_ref[slot, place]
-                    send_ref[slot, group, part] = picked
+            leaves = inside(slot)
+            if slot < 2:
+                leaves = leaves & jnp.logical_not(near(slot))
+
+            @pl.when(leaves)
+            def _():
+                pick(group, slot)
                 if relays:
                     far_way = relayed(group, slot)
 
@@ -273,28 +304,49 @@
 
         return carry
 
-    lax.fori_loop(0, groups, send_group, 0)
+    lax.fori_loop(0, FIRST_GROUPS, send_far, 0)
+    lax.fori_loop(0, groups, send_near, 0)
+    lax.fori_loop(FIRST_GROUPS, groups, send_far, 0)
 
     loads[2].wait()
+
+    def dot_t(left, right):
+        return lax.dot_general(
+            left, right, (((1,), (1,)), ((), ())), preferred_element_type=jnp.float32
+        )
 
     def own_head(head, carry):
         columns = pl.ds(pl.multiple_of(head * HD, HD), HD)
-        scores = lax.dot_general(
-            q_ref[:, columns],
-            k_ref[:, columns],
-            (((1,), (1,)), ((), ())),
-            preferred_element_type=jnp.float32,
-        )
-        peak = jnp.max(scores, axis=1, keepdims=True)
-        weights = jnp.exp2((scores - peak) * scale)
-        peak_ref[head] = peak
-        total_ref[head] = jnp.sum(weights, axis=1, keepdims=True)
-        acc_ref[:, columns] = jnp.dot(
-            weights.astype(jnp.bfloat16), v_ref[:, columns], preferred_element_type=jnp.float32
-        )
+        for slot in (0, 1):
+
+            @pl.when(near(slot) & inside(slot))
+            def _():
+                block_arrival(head, slot).wait_recv()
+
+        for start in range(0, tokens, OWN_ROWS):
+            rows = slice(start, start + OWN_ROWS)
+            queries = q_ref[rows, columns]
+            scores = dot_t(queries, k_ref[:, columns])
+            scores_near = dot_t(queries, recv_ref[head, 0, :block, :]) + bias_ref[rows, :block]
+            peak = jnp.maximum(
+                jnp.max(scores, axis=1, keepdims=True), jnp.max(scores_near, axis=1, keepdims=True)
+            )
+            weights = jnp.exp2((scores - peak) * scale)
+            weights_near = jnp.exp2((scores_near - peak) * scale)
+            peak_ref[head, rows] = peak
+            total_ref[head, rows] = jnp.sum(weights, axis=1, keepdims=True) + jnp.sum(
+                weights_near, axis=1, keepdims=True
+            )
+            acc_ref[rows, columns] = jnp.dot(
+                weights.astype(jnp.bfloat16), v_ref[:, columns], preferred_element_type=jnp.float32
+            ) + jnp.dot(
+                weights_near.astype(jnp.bfloat16),
+                recv_ref[head, 1, :block, :],
+                preferred_element_type=jnp.float32,
+            )
         return carry
 
-    lax.fori_loop(0, groups * GROUP_HEADS, own_head, 0)
+    lax.fori_loop(0, groups, own_head, 0)
 
     def out_copy(group):
         columns = pl.ds(pl.multiple_of(group * group_width, group_width), group_width)
@@ -306,34 +358,31 @@
         if relays:
             forward_group(group)
         for slot in range(SLOTS):
-
-            @pl.when(inside(slot))
+            waits = inside(slot)
+            if slot < 2:
+                waits = waits & jnp.logical_not(near(slot))
+
+            @pl.when(waits)
             def _():
                 block_arrival(group, slot).wait_recv()
 
-        for step in range(GROUP_HEADS):
-            head = group * GROUP_HEADS + step
-            columns = pl.ds(pl.multiple_of(head * HD, HD), HD)
-            far_columns = slice(step * HD, (step + 1) * HD)
-            scores = lax.dot_general(
-                q_ref[:, columns],
-                recv_ref[group, 0, :, far_columns],
-                (((1,), (1,)), ((), ())),
-                preferred_element_type=jnp.float32,
-            )
-            scores = scores + bias_ref[...]
-            own_peak = peak_ref[head]
+        columns = pl.ds(pl.multiple_of(group * HD, HD), HD)
+        for start in range(0, tokens, FAR_ROWS):
+            rows = slice(start, start + FAR_ROWS)
+            scores = dot_t(q_ref[rows, columns], recv_ref[group, 0, block:, :])
+            scores = scores + bias_ref[rows, block:]
+            own_peak = peak_ref[group, rows]
             peak = jnp.maximum(jnp.max(scores, axis=1, keepdims=True), own_peak)
             weights = jnp.exp2((scores - peak) * scale)
             shrink = jnp.exp2((own_peak - peak) * scale)
-            total = total_ref[head] * shrink + jnp.sum(weights, axis=1, keepdims=True)
+            total = total_ref[group, rows] * shrink + jnp.sum(weights, axis=1, keepdims=True)
             far = jnp.dot(
                 weights.astype(jnp.bfloat16),
-                recv_ref[group, 1, :, far_columns],
+                recv_ref[group, 1, block:, :],
                 preferred_element_type=jnp.float32,
             )
-            attended = (acc_ref[:, columns] * shrink + far) / total
-            out_ref[:, columns] = attended.astype(jnp.bfloat16)
+            attended = (acc_ref[rows, columns] * shrink + far) / total
+            out_ref[rows, columns] = attended.astype(jnp.bfloat16)
         out_copy(group).start()
         return carry
 
@@ -369,8 +418,8 @@
     per_device, slots_row = block_lists.shape
     block = tokens // per_device
     heads = width // HD
-    groups = heads // GROUP_HEADS
-    group_width = GROUP_HEADS * HD
+    groups = heads
+    group_width = HD
     far = SLOTS * block
     hbm = pl.BlockSpec(memory_space=pl.ANY)
     return pl.pallas_call(

time: 96.2 us -> 90.7 us (0.943)
  the two profiles are of different devices: /device:TPU:4 before, /device:TPU:11 now
where the time goes in v3:
time: 90.7 us; the launch traced here: 89.7 us
  Pallas kernels  86.3 us (95%)
  local copies, waits for them, and re-layouts  3.4 us (4%)
    pallas_call x1, Pallas kernels, local(): pl.pallas_call(functools.partial(kernel, size), out_shape=jax.ShapeDtypeS...  86.3 us
    unnamed x1, local copies, waits for them, and re-layouts  3.4 us

profile of v3, /device:TPU:11, one launch (start us, length us, event | category | flops | bytes accessed | tf_op | source)
XLA Modules:
  0.0 89.7 jit_solution(14569853192942753223)
XLA Ops:
  0.0 86.3 %shard_map.46 = bf16[512,2560]{1,0:T(8,128)(2,1)} custom-call(bf16[512,2560]{1,0:T(8,128)(2,1)} %q_hbm.1, bf16[512,2560]{1,0:T(8,128)(2,1)} %k_hbm.1, bf16[512,2560]{1,0:T(8,128)(2,1)} %v_hbm.1, s32[4,8]{1,0:T(4,128)} %lists_vmem.1, s32[4,8]{1,0:T(4,128)} %lists_vmem.1), custom_call_target="tpu_custom_call" | custom-call | flops 5368709120 | bytes 10485760 | tf_op jit(solution)/shard_map/pallas_call | solution.py:425
  86.3 3.4 %copy.6 = bf16[512,2560]{1,0:T(8,128)(2,1)} copy(bf16[512,2560]{1,0:T(8,128)(2,1)} %shard_map.46) | data formatting | bytes 5242880

commit v4 on v3

--- a/solution.py
+++ b/solution.py
@@ -81,8 +81,8 @@
         pltpu.make_async_copy(v_hbm, v_ref, load_sem.at[1]),
         pltpu.make_async_copy(q_hbm, q_ref, load_sem.at[2]),
     ]
-    for load in loads:
-        load.start()
+    loads[0].start()
+    loads[1].start()
 
     quads = size // QUAD
     quad = me // QUAD
@@ -180,6 +180,7 @@
         def _():
             list_arrival(slot).wait_recv()
 
+    loads[2].start()
     to_smem = pltpu.make_async_copy(named_vmem, named_smem, smem_sem)
     to_smem.start()
     to_smem.wait()
@@ -356,7 +357,11 @@
 
     def far_group(group, carry):
         if relays:
-            forward_group(group)
+
+            @pl.when(group + 1 < groups)
+            def _():
+                forward_group(group + 1)
+
         for slot in range(SLOTS):
             waits = inside(slot)
             if slot < 2:
@@ -386,6 +391,8 @@
         out_copy(group).start()
         return carry
 
+    if relays:
+        forward_group(0)
     lax.fori_loop(0, groups, far_group, 0)
 
     def finish(group, carry):

time: 90.7 us -> 90.7 us (level)
  no operation moved by 1% of the time
where the time goes in v4:
time: 90.7 us; the launch traced here: 89.7 us
  Pallas kernels  86.3 us (95%)
  local copies, waits for them, and re-layouts  3.4 us (4%)
    pallas_call x1, Pallas kernels, local(): pl.pallas_call(functools.partial(kernel, size), out_shape=jax.ShapeDtypeS...  86.3 us
    unnamed x1, local copies, waits for them, and re-layouts  3.4 us

profile of v4, /device:TPU:11, one launch (start us, length us, event | category | flops | bytes accessed | tf_op | source)
XLA Modules:
  0.0 89.7 jit_solution(2311748234799269645)
XLA Ops:
  0.0 86.3 %shard_map.46 = bf16[512,2560]{1,0:T(8,128)(2,1)} custom-call(bf16[512,2560]{1,0:T(8,128)(2,1)} %q_hbm.1, bf16[512,2560]{1,0:T(8,128)(2,1)} %k_hbm.1, bf16[512,2560]{1,0:T(8,128)(2,1)} %v_hbm.1, s32[4,8]{1,0:T(4,128)} %lists_vmem.1, s32[4,8]{1,0:T(4,128)} %lists_vmem.1), custom_call_target="tpu_custom_call" | custom-call | flops 5368709120 | bytes 10485760 | tf_op jit(solution)/shard_map/pallas_call | solution.py:432
  86.3 3.4 %copy.6 = bf16[512,2560]{1,0:T(8,128)(2,1)} copy(bf16[512,2560]{1,0:T(8,128)(2,1)} %shard_map.46) | data formatting | bytes 5242880
